TPU v7x, 32 devices: a whole 2x2x4 slice. The times are simulated.
32 devices in a mesh: grp: 2 (over y), depth: 4 (over z), shot: 2 (over x), lat: 2 (over core).
Axes of the slice: x: 2, y: 2, z: 4, core: 2. Of those that a mesh axis runs over, the one named last changes fastest.
Arguments:
- fwd_prev: float32 [8, 8, 128, 128], P(('grp', 'shot'), 'depth', 'lat'), parts along dimension 0, may hold values from -6 to 6
- fwd_now: float32 [8, 8, 128, 128], P(('grp', 'shot'), 'depth', 'lat'), parts along dimension 0, may hold values from -6 to 6
- adj_late: float32 [8, 8, 128, 128], P(('grp', 'shot'), 'depth', 'lat'), parts along dimension 0, may hold values from -6 to 6
- adj_last: float32 [8, 8, 128, 128], P(('grp', 'shot'), 'depth', 'lat'), parts along dimension 0, may hold values from -6 to 6
- velocity: float32 [16, 128, 128], P(('grp', 'depth'), 'lat', 'shot'), parts along dimension 0, may hold values from 1.5 to 4.5
- density: float32 [16, 128, 128], P(('grp', 'depth'), 'lat'), parts along dimension 0, may hold values from 1.5 to 2.5
- wavelet: float32 [8, 2], P(('grp', 'shot')), parts along dimension 0, may hold values from -48 to 48
- source_cell: int32 [8], P(('grp', 'shot')), parts along dimension 0, may hold values from 0 to 131071
- receiver_cell: int32 [8, 2048], P(('grp', 'shot')), parts along dimension 0, may hold values from 0 to 131071
- observed: float32 [8, 2, 2048], P(('grp', 'shot')), parts along dimension 0, may hold values from -18 to 18
Outputs:
- updated_velocity: float32 [16, 128, 128], P(('grp', 'depth'), 'lat', 'shot'), parts along dimension 0
- update_direction: float32 [16, 128, 128], P(('grp', 'depth'), 'lat', 'shot'), parts along dimension 0
There are 2 independent parts, one for each index of `grp`. A program takes and returns all parts, laid end to end along the dimension named above; each array names one. Nothing has to cross between parts.
Inputs may be any that keep to these rules, and one draw needn't show every extreme that they name: `source_cell`: a flattened cell index depth * 128 * 128 + x * 128 + y. `receiver_cell`: flattened cell indices depth * 128 * 128 + x * 128 + y; a cell may repeat.
All inputs are finite; a program needn't handle non-finite values. Where the computation divides by a largest or mean magnitude, that divisor is 1e-20 or more.
Results may differ from a plain program's by a relative error of at most 0.00002.
Values sent between devices are 32-bit elements; how exact they have to be, the bound alone decides.
A program may use at most 64 MiB of HBM per device.

v0:
```python
import functools

import jax
import jax.numpy as jnp
from jax import lax
from jax.experimental import pallas as pl
from jax.experimental.pallas import tpu as pltpu
from jax.sharding import PartitionSpec as P

ITERS = 2
COURANT = 0.1
STEP_SIZE = 0.1
EPSILON = 1e-06
TILE = 8
MESH = pl.DeviceIdType.MESH


def split_index(value, size):
    if size & (size - 1) == 0:
        return lax.shift_right_logical(value, size.bit_length() - 1), value & (size - 1)
    return value // size, value % size


def roll_rows(block, edge, up):
    groups, depth, rows, cols = block.shape
    flat = pltpu.roll(block.reshape(groups * depth, rows, cols), rows - 1 if up else 1, 1)
    place = lax.broadcasted_iota(jnp.int32, flat.shape, 1)
    edge = jnp.broadcast_to(edge, (groups, depth, 1, cols)).reshape(groups * depth, 1, cols)
    return jnp.where(place == (rows - 1 if up else 0), edge, flat).reshape(block.shape)


def roll_cols(block, up):
    groups, depth, rows, cols = block.shape
    flat = pltpu.roll(block.reshape(groups * depth * rows, cols), cols - 1 if up else 1, 1)
    place = lax.broadcasted_iota(jnp.int32, flat.shape, 1)
    return jnp.where(place == (cols - 1 if up else 0), 0.0, flat).reshape(block.shape)


def neighbours(block, faces):
    zlo, zhi, rlo, rhi = faces
    return (
        jnp.concatenate([block[:, 1:], zhi], axis=1),
        jnp.concatenate([zlo, block[:, :-1]], axis=1),
        roll_rows(block, rhi, True),
        roll_rows(block, rlo, False),
        roll_cols(block, True),
        roll_cols(block, False),
    )


def laplace(block, faces, weights):
    total = None
    for near, weight in zip(neighbours(block, faces), weights):
        term = weight * (near - block)
        total = term if total is None else total + term
    return total


def kernel(
    sizes,
    fwd_prev,
    fwd_now,
    adj_late,
    adj_last,
    velocity,
    density,
    wavelet,
    source,
    receiver,
    observed,
    out_velocity,
    out_direction,
    wave_z,
    wave_r,
    model_z,
    model_r,
    wave_own,
    model_own,
    grad_own,
    grad_in,
    vel_in,
    vel_line,
    max_own,
    max_in,
    wave_send,
    wave_recv,
    model_send,
    model_recv,
    shot_send,
    shot_recv,
    max_send,
    max_recv,
):
    depth_n, shot_n, lat_n = sizes
    shots, depth, rows, cols = fwd_now.shape
    steps = observed.shape[1]
    count = receiver.shape[1]
    width = velocity.shape[2]
    me_z, me_s, me_l = lax.axis_index("depth"), lax.axis_index("shot"), lax.axis_index("lat")
    group = depth_n * lat_n
    me_g = me_z * lat_n + me_l

    def group_peer(offset):
        other = lax.rem(me_g + offset, group)
        return {"depth": other // lat_n, "lat": lax.rem(other, lat_n)}

    def shot_peer(offset):
        return {"shot": lax.rem(me_s + offset, shot_n)}

    barrier = pltpu.get_barrier_semaphore()
    for offset in range(1, group):
        pl.semaphore_signal(barrier, inc=1, device_id=group_peer(offset), device_id_type=MESH)
    for offset in range(1, shot_n):
        pl.semaphore_signal(barrier, inc=1, device_id=shot_peer(offset), device_id_type=MESH)
    pl.semaphore_wait(barrier, group - 1 + shot_n - 1)

    sides = (
        (me_z > 0, {"depth": me_z - 1}, me_z < depth_n - 1),
        (me_z < depth_n - 1, {"depth": me_z + 1}, me_z > 0),
        (me_l > 0, {"lat": me_l - 1}, me_l < lat_n - 1),
        (me_l < lat_n - 1, {"lat": me_l + 1}, me_l > 0),
    )

    def face_copies(src, zbuf, rbuf, send, recv, slot):
        refs = (
            (src.at[:, 0:1], zbuf.at[slot, 1]),
            (src.at[:, depth - 1 : depth], zbuf.at[slot, 0]),
            (src.at[:, :, 0:TILE], rbuf.at[slot, 1]),
            (src.at[:, :, rows - TILE : rows], rbuf.at[slot, 0]),
        )
        return [
            pltpu.make_async_remote_copy(
                src_ref=here,
                dst_ref=there,
                send_sem=send.at[slot, way],
                recv_sem=recv.at[slot, way],
                device_id=sides[way][1],
                device_id_type=MESH,
            )
            for way, (here, there) in enumerate(refs)
        ]

    pending = []

    def start_faces(src, is_wave, slot):
        if is_wave:
            copies = face_copies(src, wave_z, wave_r, wave_send, wave_recv, slot)
        else:
            copies = face_copies(src, model_z, model_r, model_send, model_recv, slot)
        for way, copy in enumerate(copies):
            pl.when(sides[way][0])(copy.start)
            pending.append((sides[way][0], copy))
        return copies

    def wait_faces(copies):
        for way, copy in enumerate(copies):
            pl.when(sides[way][2])(copy.wait_recv)

    def read_faces(is_wave, slot):
        zbuf, rbuf = (wave_z, wave_r) if is_wave else (model_z, model_r)
        return (
            jnp.where(me_z > 0, zbuf[slot, 0], 0.0),
            jnp.where(me_z < depth_n - 1, zbuf[slot, 1], 0.0),
            jnp.where(me_l > 0, rbuf[slot, 0][:, :, TILE - 1 : TILE], 0.0),
            jnp.where(me_l < lat_n - 1, rbuf[slot, 1][:, :, 0:1], 0.0),
        )

    def shot_copies(src, buffer, slot):
        return [
            pltpu.make_async_remote_copy(
                src_ref=src,
                dst_ref=buffer.at[offset - 1],
                send_sem=shot_send.at[slot, offset - 1],
                recv_sem=shot_recv.at[slot, offset - 1],
                device_id=shot_peer(offset),
                device_id_type=MESH,
            )
            for offset in range(1, shot_n)
        ]

    vel_copies = shot_copies(velocity, vel_in, 0)
    for copy in vel_copies:
        copy.start()
    density_copies = start_faces(density, False, 0)
    now_copies = start_faces(fwd_now, True, 0)
    last_copies = start_faces(adj_last, True, 1)

    plane_start = me_z * depth
    row_start = me_l * rows
    full_rows = rows * lat_n
    counts = []
    records = [[] for unused in range(steps)]
    row_place = lax.broadcasted_iota(jnp.int32, (depth * rows, count), 0)
    col_place = lax.broadcasted_iota(jnp.int32, (cols, count), 0)
    for shot in range(shots):
        line, col = split_index(receiver[shot : shot + 1, :], cols)
        plane, row = split_index(line, full_rows)
        plane = plane - plane_start
        row = row - row_start
        inside = (plane >= 0) & (plane < depth) & (row >= 0) & (row < rows)
        place = jnp.where(inside, plane * rows + row, -1)
        picks = jnp.where(row_place == place, 1.0, 0.0)
        col_picks = jnp.where(col_place == col, 1.0, 0.0).astype(jnp.bfloat16)

        def spread(values, picks=picks, col_picks=col_picks):
            left = picks if values is None else picks * values
            return lax.dot_general(
                left.astype(jnp.bfloat16),
                col_picks,
                (((1,), (1,)), ((), ())),
                preferred_element_type=jnp.float32,
            )

        counts.append(spread(None).reshape(1, depth, rows, cols))
        for step in range(steps):
            value = observed[shot, step : step + 1, :]
            high = value.astype(jnp.bfloat16).astype(jnp.float32)
            middle = (value - high).astype(jnp.bfloat16).astype(jnp.float32)
            low = value - high - middle
            total = spread(high) + (spread(middle) + spread(low))
            records[step].append(total.reshape(1, depth, rows, cols))
    counts = jnp.concatenate(counts, axis=0)
    records = [jnp.concatenate(record, axis=0) for record in records]

    spot = (1, depth, rows, cols)
    cell_index = (
        (lax.broadcasted_iota(jnp.int32, spot, 1) + plane_start) * full_rows
        + lax.broadcasted_iota(jnp.int32, spot, 2)
        + row_start
    ) * cols + lax.broadcasted_iota(jnp.int32, spot, 3)
    hits = [cell_index == source[shot] for shot in range(shots)]

    def sources(step):
        return jnp.concatenate(
            [jnp.where(hits[shot], wavelet[shot, step], 0.0) for shot in range(shots)], axis=0
        )

    def placed(piece, owner):
        vel_line[:, :, 0:width] = piece
        line = vel_line[...].reshape(depth * rows, cols)
        return pltpu.roll(line, owner * width, 1).reshape(depth, rows, cols)

    vel_line[...] = jnp.zeros_like(vel_line)
    speed = placed(velocity[...], me_s)
    for offset in range(1, shot_n):
        vel_copies[offset - 1].wait_recv()
        speed = speed + placed(vel_in[offset - 1], lax.rem(me_s + shot_n - offset, shot_n))

    wait_faces(density_copies)
    own_density = density[...]
    dens_faces = read_faces(False, 0)
    valid = (me_z > 0, me_z < depth_n - 1, me_l > 0, me_l < lat_n - 1)
    buoy = 1.0 / own_density
    buoy_faces = tuple(
        jnp.where(ok, 1.0 / jnp.where(ok, face, 1.0), 0.0) for ok, face in zip(valid, dens_faces)
    )
    weights = [0.5 * (buoy + near) for near in neighbours(buoy, buoy_faces)]

    wait_faces(now_copies)
    first = fwd_now[...]
    before = fwd_prev[...]
    first_lap = laplace(first, read_faces(True, 0), weights)
    wait_faces(last_copies)
    last = adj_last[...]
    late = adj_late[...]
    last_faces = read_faces(True, 1)

    direction = None
    wave_slot = 2
    for update in range(ITERS):
        stiff = (speed[None] * COURANT) ** 2 * own_density
        model_own[update] = stiff
        stiff_copies = start_faces(model_own.at[update], False, 1 + update)
        laps = []
        misfits = []
        wave_prev, wave_now = before, first
        for step in range(steps):
            if step == 0:
                lap = first_lap
            else:
                wait_faces(wave_copies)
                lap = laplace(wave_now, read_faces(True, wave_slot - 1), weights)
            wave_next = 2.0 * wave_now - wave_prev + stiff * lap + sources(step)
            if step < steps - 1:
                wave_own[wave_slot - 2] = wave_next
                wave_copies = start_faces(wave_own.at[wave_slot - 2], True, wave_slot)
                wave_slot += 1
            laps.append(lap)
            misfits.append(counts * wave_next - records[step])
            wave_prev, wave_now = wave_now, wave_next
            if step == 0:
                wait_faces(stiff_copies)
                stiff_faces = read_faces(False, 1 + update)
                scaled = stiff * last
                scaled_faces = tuple(a * b for a, b in zip(stiff_faces, last_faces))
                scaled_lap = laplace(scaled, scaled_faces, weights)
        gradient = None
        adj_late_now, adj_now = late, last
        for step in reversed(range(steps)):
            if step < steps - 1:
                wait_faces(wave_copies)
                scaled_lap = laplace(scaled, read_faces(True, wave_slot - 1), weights)
            adj_next = 2.0 * adj_now - adj_late_now + scaled_lap + misfits[step]
            scaled = stiff * adj_next
            if step > 0:
                wave_own[wave_slot - 2] = scaled
                wave_copies = start_faces(wave_own.at[wave_slot - 2], True, wave_slot)
                wave_slot += 1
            term = jnp.sum(scaled * laps[step], axis=0)
            gradient = term if gradient is None else gradient + term
            adj_late_now, adj_now = adj_now, adj_next
        grad_own[update] = gradient
        grad_copies = shot_copies(grad_own.at[update], grad_in.at[update], 1 + update)
        for copy in grad_copies:
            copy.start()
        for offset, copy in enumerate(grad_copies):
            copy.wait_recv()
            gradient = gradient + grad_in[update, offset]
        top = jnp.max(jnp.abs(gradient).reshape(-1, TILE, cols), axis=0)
        max_own[update] = top
        max_copies = [
            pltpu.make_async_remote_copy(
                src_ref=max_own.at[update],
                dst_ref=max_in.at[update, offset - 1],
                send_sem=max_send.at[update, offset - 1],
                recv_sem=max_recv.at[update, offset - 1],
                device_id=group_peer(offset),
                device_id_type=MESH,
            )
            for offset in range(1, group)
        ]
        for copy in max_copies:
            copy.start()
        for offset, copy in enumerate(max_copies):
            copy.wait_recv()
            top = jnp.maximum(top, max_in[update, offset])
        largest = jnp.max(top)
        direction = gradient / (largest + EPSILON)
        speed = speed * jnp.exp(-STEP_SIZE * direction)
        for copy in grad_copies + max_copies:
            copy.wait_send()

    def own_lines(block):
        flat = block.reshape(depth * rows, cols)
        turned = pltpu.roll(flat, lax.rem(cols - me_s * width, cols), 1)
        return turned[:, 0:width].reshape(depth, rows, width)

    out_velocity[...] = own_lines(speed)
    out_direction[...] = own_lines(direction)
    for copy in vel_copies:
        copy.wait_send()
    for going, copy in pending:
        pl.when(going)(copy.wait_send)


def shards(sizes, *arrays):
    velocity = arrays[4]
    shots, depth, rows, cols = arrays[1].shape
    steps = arrays[6].shape[1]
    depth_n, shot_n, lat_n = sizes
    arrays = list(arrays)
    arrays[5] = arrays[5][None]
    waves = 2 + ITERS * 2 * (steps - 1)
    models = 1 + ITERS
    group = depth_n * lat_n
    f32 = jnp.float32
    dma = pltpu.SemaphoreType.DMA
    vmem = pl.BlockSpec(memory_space=pltpu.VMEM)
    smem = pl.BlockSpec(memory_space=pltpu.SMEM)
    peers = max(shot_n - 1, 1)
    others = max(group - 1, 1)
    out = jax.ShapeDtypeStruct(velocity.shape, f32)
    return pl.pallas_call(
        functools.partial(kernel, sizes),
        out_shape=(out, out),
        in_specs=[vmem] * 6 + [smem] * 2 + [vmem] * 2,
        out_specs=(vmem, vmem),
        scratch_shapes=[
            pltpu.VMEM((waves, 2, shots, 1, rows, cols), f32),
            pltpu.VMEM((waves, 2, shots, depth, TILE, cols), f32),
            pltpu.VMEM((models, 2, 1, 1, rows, cols), f32),
            pltpu.VMEM((models, 2, 1, depth, TILE, cols), f32),
            pltpu.VMEM((max(waves - 2, 1), shots, depth, rows, cols), f32),
            pltpu.VMEM((ITERS, 1, depth, rows, cols), f32),
            pltpu.VMEM((ITERS, depth, rows, cols), f32),
            pltpu.VMEM((ITERS, peers, depth, rows, cols), f32),
            pltpu.VMEM((peers,) + velocity.shape, f32),
            pltpu.VMEM((depth, rows, cols), f32),
            pltpu.VMEM((ITERS, TILE, cols), f32),
            pltpu.VMEM((ITERS, others, TILE, cols), f32),
            dma((waves, 4)),
            dma((waves, 4)),
            dma((models, 4)),
            dma((models, 4)),
            dma((1 + ITERS, peers)),
            dma((1 + ITERS, peers)),
            dma((ITERS, others)),
            dma((ITERS, others)),
        ],
        compiler_params=pltpu.CompilerParams(
            collective_id=0, has_side_effects=True, vmem_limit_bytes=32 * 1024 * 1024
        ),
    )(*arrays)


def solution(mesh):
    sizes = (mesh.shape["depth"], mesh.shape["shot"], mesh.shape["lat"])
    placed = (
        P(("grp", "shot"), "depth", "lat", None),
        P(("grp", "shot"), "depth", "lat", None),
        P(("grp", "shot"), "depth", "lat", None),
        P(("grp", "shot"), "depth", "lat", None),
        P(("grp", "depth"), "lat", "shot"),
        P(("grp", "depth"), "lat", None),
        P(("grp", "shot"), None),
        P(("grp", "shot")),
        P(("grp", "shot"), None),
        P(("grp", "shot"), None, None),
    )
    return jax.shard_map(
        functools.partial(shards, sizes),
        mesh=mesh,
        in_specs=placed,
        out_specs=(P(("grp", "depth"), "lat", "shot"), P(("grp", "depth"), "lat", "shot")),
        check_vma=False,
    )
```

profile of v0, /device:TPU:0, one launch (start us, length us, event | category | flops | bytes accessed | tf_op | source)
XLA Modules:
  0.0 50.2 jit_solution(2702309615901754297)
XLA Ops:
  0.6 0.0 copy-start.9
  0.6 0.0 copy-start.8
  0.7 0.6 %copy-done.9 = s32[2]{0:T(128)S(1)} copy-done((s32[2]{0:T(128)S(1)}, s32[2]{0:T(128)}, u32[]{:S(2)}) %copy-start.9) | copy-done | bytes 32
  1.3 0.0 copy-done.8
  1.3 0.0 copy-start
  1.3 0.9 %copy-done = f32[2,2,64,128]{3,2,1,0:T(8,128)S(1)} copy-done((f32[2,2,64,128]{3,2,1,0:T(8,128)S(1)}, f32[2,2,64,128]{3,2,1,0:T(8,128)}, u32[]{:S(2)}) %copy-start) | copy-done | bytes 131096
  2.2 0.0 copy-start.1
  2.2 0.9 %copy-done.1 = f32[2,2,64,128]{3,2,1,0:T(8,128)S(1)} copy-done((f32[2,2,64,128]{3,2,1,0:T(8,128)S(1)}, f32[2,2,64,128]{3,2,1,0:T(8,128)}, u32[]{:S(2)}) %copy-start.1) | copy-done | bytes 131096
  3.1 0.0 copy-start.2
  3.1 0.9 %copy-done.2 = f32[2,2,64,128]{3,2,1,0:T(8,128)S(1)} copy-done((f32[2,2,64,128]{3,2,1,0:T(8,128)S(1)}, f32[2,2,64,128]{3,2,1,0:T(8,128)}, u32[]{:S(2)}) %copy-start.2) | copy-done | bytes 131096
  4.0 0.0 copy-start.3
  4.0 0.9 %copy-done.3 = f32[2,2,64,128]{3,2,1,0:T(8,128)S(1)} copy-done((f32[2,2,64,128]{3,2,1,0:T(8,128)S(1)}, f32[2,2,64,128]{3,2,1,0:T(8,128)}, u32[]{:S(2)}) %copy-start.3) | copy-done | bytes 131096
  4.9 0.0 copy-start.4
  5.0 0.8 %copy-done.4 = f32[2,64,64]{2,1,0:T(8,128)S(1)} copy-done((f32[2,64,64]{2,1,0:T(8,128)S(1)}, f32[2,64,64]{2,1,0:T(8,128)}, u32[]{:S(2)}) %copy-start.4) | copy-done | bytes 32792
  5.8 0.0 copy-start.5
  5.8 0.8 %copy-done.5 = f32[2,64,128]{2,1,0:T(8,128)S(1)} copy-done((f32[2,64,128]{2,1,0:T(8,128)S(1)}, f32[2,64,128]{2,1,0:T(8,128)}, u32[]{:S(2)}) %copy-start.5) | copy-done | bytes 65560
  6.6 0.0 copy-start.6
  6.6 0.8 %copy-done.6 = f32[2,2,2048]{2,1,0:T(2,128)S(1)} copy-done((f32[2,2,2048]{2,1,0:T(2,128)S(1)}, f32[2,2,2048]{2,1,0:T(2,128)}, u32[]{:S(2)}) %copy-start.6) | copy-done | bytes 32792
  7.4 0.0 copy-start.7
  7.4 0.7 %copy-done.7 = s32[2,2048]{1,0:T(2,128)S(1)} copy-done((s32[2,2048]{1,0:T(2,128)S(1)}, s32[2,2048]{1,0:T(2,128)}, u32[]{:S(2)}) %copy-start.7) | copy-done | bytes 16408
  8.1 40.8 %shard_map.113 = (f32[2,64,64]{2,1,0:T(8,128)S(1)}, f32[2,64,64]{2,1,0:T(8,128)S(1)}) custom-call(f32[2,2,64,128]{3,2,1,0:T(8,128)S(1)} %copy-done, f32[2,2,64,128]{3,2,1,0:T(8,128)S(1)} %copy-done.1, f32[2,2,64,128]{3,2,1,0:T(8,128)S(1)} %copy-done.2, f32[2,2,64,128]{3,2,1,0:T(8,128)S(1)} %copy-done.3, f32[2,64,64]{2,1,0:T(8,128)S(1)} %copy-done.4, ...), custom_call_target="tpu_custom_call" | custom-call | tf_op jit(solution)/shard_map/pallas_call | solution.py:373
  48.9 0.6 %copy.14 = f32[2,64,64]{2,1,0:T(8,128)} copy(f32[2,64,64]{2,1,0:T(8,128)S(1)} %get-tuple-element.4) | data formatting | bytes 65536
  49.6 0.6 %copy.15 = f32[2,64,64]{2,1,0:T(8,128)} copy(f32[2,64,64]{2,1,0:T(8,128)S(1)} %get-tuple-element.5) | data formatting | bytes 65536
Async XLA Ops:
  0.6 0.7 %copy-start.9 = (s32[2]{0:T(128)S(1)}, s32[2]{0:T(128)}, u32[]{:S(2)}) copy-start(s32[2]{0:T(128)} %source.1) | copy-start | bytes 28
  0.6 0.7 %copy-start.8 = (f32[2,2]{1,0:T(2,128)S(1)}, f32[2,2]{1,0:T(2,128)}, u32[]{:S(2)}) copy-start(f32[2,2]{1,0:T(2,128)} %wavelet.1) | copy-start | bytes 52
  1.3 0.9 %copy-start = (f32[2,2,64,128]{3,2,1,0:T(8,128)S(1)}, f32[2,2,64,128]{3,2,1,0:T(8,128)}, u32[]{:S(2)}) copy-start(f32[2,2,64,128]{3,2,1,0:T(8,128)} %fwd_prev.1) | copy-start | bytes 393220
  2.2 0.9 %copy-start.1 = (f32[2,2,64,128]{3,2,1,0:T(8,128)S(1)}, f32[2,2,64,128]{3,2,1,0:T(8,128)}, u32[]{:S(2)}) copy-start(f32[2,2,64,128]{3,2,1,0:T(8,128)} %fwd_now.1) | copy-start | bytes 393220
  3.1 0.9 %copy-start.2 = (f32[2,2,64,128]{3,2,1,0:T(8,128)S(1)}, f32[2,2,64,128]{3,2,1,0:T(8,128)}, u32[]{:S(2)}) copy-start(f32[2,2,64,128]{3,2,1,0:T(8,128)} %adj_late.1) | copy-start | bytes 393220
  4.0 0.9 %copy-start.3 = (f32[2,2,64,128]{3,2,1,0:T(8,128)S(1)}, f32[2,2,64,128]{3,2,1,0:T(8,128)}, u32[]{:S(2)}) copy-start(f32[2,2,64,128]{3,2,1,0:T(8,128)} %adj_last.1) | copy-start | bytes 393220
  4.9 0.8 %copy-start.4 = (f32[2,64,64]{2,1,0:T(8,128)S(1)}, f32[2,64,64]{2,1,0:T(8,128)}, u32[]{:S(2)}) copy-start(f32[2,64,64]{2,1,0:T(8,128)} %velocity.1) | copy-start | bytes 98308
  5.8 0.8 %copy-start.5 = (f32[2,64,128]{2,1,0:T(8,128)S(1)}, f32[2,64,128]{2,1,0:T(8,128)}, u32[]{:S(2)}) copy-start(f32[2,64,128]{2,1,0:T(8,128)} %param.15) | copy-start | bytes 196612
  6.6 0.8 %copy-start.6 = (f32[2,2,2048]{2,1,0:T(2,128)S(1)}, f32[2,2,2048]{2,1,0:T(2,128)}, u32[]{:S(2)}) copy-start(f32[2,2,2048]{2,1,0:T(2,128)} %observed.1) | copy-start | bytes 98308
  7.4 0.7 %copy-start.7 = (s32[2,2048]{1,0:T(2,128)S(1)}, s32[2,2048]{1,0:T(2,128)}, u32[]{:S(2)}) copy-start(s32[2,2048]{1,0:T(2,128)} %receiver.1) | copy-start | bytes 49156
where the time goes:
time: 50.6 us; the launch traced here: 50.2 us
  Pallas kernels  40.8 us (81%)
  local copies, waits for them, and re-layouts  8.71 us (17%)
  between operations  0.67 us (1%)
    pallas_call x1, Pallas kernels, shards(): pl.pallas_call(functools.partial(kernel, sizes), out_shape=(out, out), in...  40.8 us
    unnamed x22, local copies, waits for them, and re-layouts  8.71 us

commit v1 on v0

--- a/solution.py
+++ b/solution.py
@@ -48,6 +48,27 @@
     )
 
 
+def inner_laplace(block, weights):
+    depth_zero = jnp.zeros_like(block[:, 0:1])
+    row_zero = jnp.zeros_like(block[:, :, 0:1])
+    return laplace(block, (depth_zero, depth_zero, row_zero, row_zero), weights)
+
+
+def add_faces(inner, faces, weights):
+    zlo, zhi, rlo, rhi = faces
+    high, low, up, down = weights[:4]
+    depth, rows = inner.shape[1:3]
+    place = lax.broadcasted_iota(jnp.int32, (1, 1, TILE, inner.shape[3]), 2)
+    first = inner[:, :, :TILE] + jnp.where(place == 0, down[:, :, :TILE] * rlo, 0.0)
+    inner = jnp.concatenate([first, inner[:, :, TILE:]], axis=2)
+    last = inner[:, :, rows - TILE :]
+    last = last + jnp.where(place == TILE - 1, up[:, :, rows - TILE :] * rhi, 0.0)
+    inner = jnp.concatenate([inner[:, :, : rows - TILE], last], axis=2)
+    inner = jnp.concatenate([inner[:, :1] + low[:, :1] * zlo, inner[:, 1:]], axis=1)
+    last = inner[:, depth - 1 :] + high[:, depth - 1 :] * zhi
+    return jnp.concatenate([inner[:, : depth - 1], last], axis=1) if depth > 1 else last
+
+
 def laplace(block, faces, weights):
     total = None
     for near, weight in zip(neighbours(block, faces), weights):
@@ -58,6 +79,17 @@
 
 def kernel(
     sizes,
+    fwd_prev_hbm,
+    fwd_now_hbm,
+    adj_late_hbm,
+    adj_last_hbm,
+    velocity_hbm,
+    density_hbm,
+    wavelet_hbm,
+    source_hbm,
+    receiver_hbm,
+    observed_hbm,
+    out_pair,
     fwd_prev,
     fwd_now,
     adj_late,
@@ -68,8 +100,7 @@
     source,
     receiver,
     observed,
-    out_velocity,
-    out_direction,
+    load_sem,
     wave_z,
     wave_r,
     model_z,
@@ -107,6 +138,24 @@
     def shot_peer(offset):
         return {"shot": lax.rem(me_s + offset, shot_n)}
 
+    loads = {}
+    for place, (name, there, here) in enumerate(
+        (
+            ("receiver", receiver_hbm, receiver),
+            ("observed", observed_hbm, observed),
+            ("velocity", velocity_hbm, velocity),
+            ("density", density_hbm, density),
+            ("fwd_now", fwd_now_hbm, fwd_now),
+            ("fwd_prev", fwd_prev_hbm, fwd_prev),
+            ("adj_last", adj_last_hbm, adj_last),
+            ("adj_late", adj_late_hbm, adj_late),
+            ("wavelet", wavelet_hbm, wavelet),
+            ("source", source_hbm, source),
+        )
+    ):
+        loads[name] = pltpu.make_async_copy(there, here, load_sem.at[place])
+        loads[name].start()
+
     barrier = pltpu.get_barrier_semaphore()
     for offset in range(1, group):
         pl.semaphore_signal(barrier, inc=1, device_id=group_peer(offset), device_id_type=MESH)
@@ -178,12 +227,14 @@
             for offset in range(1, shot_n)
         ]
 
-    vel_copies = shot_copies(velocity, vel_in, 0)
+    vel_copies = shot_copies(velocity_hbm, vel_in, 0)
     for copy in vel_copies:
         copy.start()
-    density_copies = start_faces(density, False, 0)
-    now_copies = start_faces(fwd_now, True, 0)
-    last_copies = start_faces(adj_last, True, 1)
+    density_copies = start_faces(density_hbm, False, 0)
+    now_copies = start_faces(fwd_now_hbm, True, 0)
+    last_copies = start_faces(adj_last_hbm, True, 1)
+    loads["receiver"].wait()
+    loads["observed"].wait()
 
     plane_start = me_z * depth
     row_start = me_l * rows
@@ -228,6 +279,8 @@
         + lax.broadcasted_iota(jnp.int32, spot, 2)
         + row_start
     ) * cols + lax.broadcasted_iota(jnp.int32, spot, 3)
+    loads["source"].wait()
+    loads["wavelet"].wait()
     hits = [cell_index == source[shot] for shot in range(shots)]
 
     def sources(step):
@@ -241,12 +294,16 @@
         return pltpu.roll(line, owner * width, 1).reshape(depth, rows, cols)
 
     vel_line[...] = jnp.zeros_like(vel_line)
+    loads["velocity"].wait()
     speed = placed(velocity[...], me_s)
     for offset in range(1, shot_n):
         vel_copies[offset - 1].wait_recv()
         speed = speed + placed(vel_in[offset - 1], lax.rem(me_s + shot_n - offset, shot_n))
 
+    model_own[0] = speed[None]
+    speed_copies = start_faces(model_own.at[0], False, 1)
     wait_faces(density_copies)
+    loads["density"].wait()
     own_density = density[...]
     dens_faces = read_faces(False, 0)
     valid = (me_z > 0, me_z < depth_n - 1, me_l > 0, me_l < lat_n - 1)
@@ -256,56 +313,93 @@
     )
     weights = [0.5 * (buoy + near) for near in neighbours(buoy, buoy_faces)]
 
-    wait_faces(now_copies)
+    loads["fwd_now"].wait()
+    loads["fwd_prev"].wait()
     first = fwd_now[...]
     before = fwd_prev[...]
-    first_lap = laplace(first, read_faces(True, 0), weights)
-    wait_faces(last_copies)
+    inner = inner_laplace(first, weights)
+    wait_faces(now_copies)
+    first_lap = add_faces(inner, read_faces(True, 0), weights)
+    loads["adj_last"].wait()
+    loads["adj_late"].wait()
     last = adj_last[...]
     late = adj_late[...]
-    last_faces = read_faces(True, 1)
 
     direction = None
     wave_slot = 2
     for update in range(ITERS):
         stiff = (speed[None] * COURANT) ** 2 * own_density
-        model_own[update] = stiff
-        stiff_copies = start_faces(model_own.at[update], False, 1 + update)
+        if update > 0:
+            stiff_faces = tuple(
+                (face * COURANT) ** 2 * near for face, near in zip(speed_faces, dens_faces)
+            )
         laps = []
         misfits = []
         wave_prev, wave_now = before, first
         for step in range(steps):
             if step == 0:
                 lap = first_lap
+            elif step == 1 and update == 0:
+                wait_faces(wave_copies)
+                second_faces = read_faces(True, second_slot)
+                lap = add_faces(inner, second_faces, weights)
+            elif step == 1:
+                if update == 1:
+                    wait_faces(lap_copies)
+                    lap_faces = read_faces(True, second_slot + 1)
+                near = tuple(
+                    old + (stiff_face - stiff_old) * lap_face
+                    for old, stiff_face, stiff_old, lap_face in zip(
+                        second_faces, stiff_faces, first_stiff_faces, lap_faces
+                    )
+                )
+                lap = add_faces(inner, near, weights)
             else:
                 wait_faces(wave_copies)
-                lap = laplace(wave_now, read_faces(True, wave_slot - 1), weights)
+                lap = add_faces(inner, read_faces(True, wave_slot - 1), weights)
             wave_next = 2.0 * wave_now - wave_prev + stiff * lap + sources(step)
-            if step < steps - 1:
+            if step < steps - 1 and (step > 0 or update == 0):
                 wave_own[wave_slot - 2] = wave_next
                 wave_copies = start_faces(wave_own.at[wave_slot - 2], True, wave_slot)
                 wave_slot += 1
+                if step == 0:
+                    second_slot = wave_slot - 1
+                    wave_own[wave_slot - 2] = first_lap
+                    lap_copies = start_faces(wave_own.at[wave_slot - 2], True, wave_slot)
+                    wave_slot += 1
+            if step < steps - 1:
+                inner = inner_laplace(wave_next, weights)
             laps.append(lap)
             misfits.append(counts * wave_next - records[step])
             wave_prev, wave_now = wave_now, wave_next
             if step == 0:
-                wait_faces(stiff_copies)
-                stiff_faces = read_faces(False, 1 + update)
                 scaled = stiff * last
+                scaled_lap = inner_laplace(scaled, weights)
+                if update == 0:
+                    wait_faces(speed_copies)
+                    speed_faces = read_faces(False, 1)
+                    stiff_faces = tuple(
+                        (face * COURANT) ** 2 * near for face, near in zip(speed_faces, dens_faces)
+                    )
+                    first_stiff_faces = stiff_faces
+                    wait_faces(last_copies)
+                    last_faces = read_faces(True, 1)
                 scaled_faces = tuple(a * b for a, b in zip(stiff_faces, last_faces))
-                scaled_lap = laplace(scaled, scaled_faces, weights)
+                scaled_lap = add_faces(scaled_lap, scaled_faces, weights)
         gradient = None
         adj_late_now, adj_now = late, last
         for step in reversed(range(steps)):
+            adj_next = 2.0 * adj_now - adj_late_now + scaled_lap + misfits[step]
             if step < steps - 1:
                 wait_faces(wave_copies)
-                scaled_lap = laplace(scaled, read_faces(True, wave_slot - 1), weights)
-            adj_next = 2.0 * adj_now - adj_late_now + scaled_lap + misfits[step]
+                adj_next = add_faces(adj_next, read_faces(True, wave_slot - 1), weights)
             scaled = stiff * adj_next
             if step > 0:
                 wave_own[wave_slot - 2] = scaled
                 wave_copies = start_faces(wave_own.at[wave_slot - 2], True, wave_slot)
                 wave_slot += 1
+            if step > 0:
+                scaled_lap = inner_laplace(scaled, weights)
             term = jnp.sum(scaled * laps[step], axis=0)
             gradient = term if gradient is None else gradient + term
             adj_late_now, adj_now = adj_now, adj_next
@@ -331,12 +425,21 @@
         ]
         for copy in max_copies:
             copy.start()
+        if update < ITERS - 1:
+            model_own[1 + update] = gradient[None]
+            side_copies = start_faces(model_own.at[1 + update], False, 2 + update)
         for offset, copy in enumerate(max_copies):
             copy.wait_recv()
             top = jnp.maximum(top, max_in[update, offset])
         largest = jnp.max(top)
         direction = gradient / (largest + EPSILON)
         speed = speed * jnp.exp(-STEP_SIZE * direction)
+        if update < ITERS - 1:
+            wait_faces(side_copies)
+            speed_faces = tuple(
+                face * jnp.exp(-STEP_SIZE * (side / (largest + EPSILON)))
+                for face, side in zip(speed_faces, read_faces(False, 2 + update))
+            )
         for copy in grad_copies + max_copies:
             copy.wait_send()
 
@@ -345,12 +448,23 @@
         turned = pltpu.roll(flat, lax.rem(cols - me_s * width, cols), 1)
         return turned[:, 0:width].reshape(depth, rows, width)
 
-    out_velocity[...] = own_lines(speed)
-    out_direction[...] = own_lines(direction)
+    out_pair[0] = own_lines(speed)
+    out_pair[1] = own_lines(direction)
     for copy in vel_copies:
         copy.wait_send()
     for going, copy in pending:
         pl.when(going)(copy.wait_send)
+
+
+def finish(pair, out_velocity, out_direction, sems):
+    copies = [
+        pltpu.make_async_copy(pair.at[0], out_velocity, sems.at[0]),
+        pltpu.make_async_copy(pair.at[1], out_direction, sems.at[1]),
+    ]
+    for copy in copies:
+        copy.start()
+    for copy in copies:
+        copy.wait()
 
 
 def shards(sizes, *arrays):
@@ -360,22 +474,28 @@
     depth_n, shot_n, lat_n = sizes
     arrays = list(arrays)
     arrays[5] = arrays[5][None]
-    waves = 2 + ITERS * 2 * (steps - 1)
+    waves = 4 + ITERS * 2 * (steps - 1) - ITERS
     models = 1 + ITERS
     group = depth_n * lat_n
     f32 = jnp.float32
     dma = pltpu.SemaphoreType.DMA
     vmem = pl.BlockSpec(memory_space=pltpu.VMEM)
-    smem = pl.BlockSpec(memory_space=pltpu.SMEM)
+    hbm = pl.BlockSpec(memory_space=pltpu.HBM)
+    held = [
+        (pltpu.SMEM if place in (6, 7) else pltpu.VMEM)(array.shape, array.dtype)
+        for place, array in enumerate(arrays)
+    ]
     peers = max(shot_n - 1, 1)
     others = max(group - 1, 1)
     out = jax.ShapeDtypeStruct(velocity.shape, f32)
-    return pl.pallas_call(
+    pair = pl.pallas_call(
         functools.partial(kernel, sizes),
-        out_shape=(out, out),
-        in_specs=[vmem] * 6 + [smem] * 2 + [vmem] * 2,
-        out_specs=(vmem, vmem),
-        scratch_shapes=[
+        out_shape=jax.ShapeDtypeStruct((2,) + velocity.shape, f32),
+        in_specs=[hbm] * len(arrays),
+        out_specs=vmem,
+        scratch_shapes=held
+        + [
+            dma((len(arrays),)),
             pltpu.VMEM((waves, 2, shots, 1, rows, cols), f32),
             pltpu.VMEM((waves, 2, shots, depth, TILE, cols), f32),
             pltpu.VMEM((models, 2, 1, 1, rows, cols), f32),
@@ -398,9 +518,17 @@
             dma((ITERS, others)),
         ],
         compiler_params=pltpu.CompilerParams(
-            collective_id=0, has_side_effects=True, vmem_limit_bytes=32 * 1024 * 1024
+            collective_id=0, has_side_effects=True, vmem_limit_bytes=60 * 1024 * 1024
         ),
     )(*arrays)
+    return pl.pallas_call(
+        finish,
+        out_shape=(out, out),
+        in_specs=[vmem],
+        out_specs=(hbm, hbm),
+        scratch_shapes=[dma((2,))],
+        compiler_params=pltpu.CompilerParams(has_side_effects=True),
+    )(pair)
 
 
 def solution(mesh):

time: 50.6 us -> 38.8 us (0.77)
  local copies, waits for them, and re-layouts: 8.71 us -> 0 us
  Pallas kernels: 40.8 us -> 38 us
    unnamed x22 -> x0, local copies, waits for them, and re-layouts: 8.71 us -> none
    pallas_call x1 -> x2, Pallas kernels: 40.8 us -> 38 us  [the longest x1 36.4 us: shards(): pl.pallas_call(functools.partial(kernel, sizes), out_shape=jax.ShapeDtype...]
where the time goes in v1:
time: 38.8 us; the launch traced here: 38.6 us
  Pallas kernels  38 us (98%)
  between operations  0.64 us (2%)
    pallas_call x1, Pallas kernels, shards(): pl.pallas_call(functools.partial(kernel, sizes), out_shape=jax.ShapeDtype...  36.4 us
    pallas_call x1, Pallas kernels, shards(): pl.pallas_call(finish, out_shape=(out, out), in_specs=[vmem], out_specs=(...  1.57 us

profile of v1, /device:TPU:0, one launch (start us, length us, event | category | flops | bytes accessed | tf_op | source)
XLA Modules:
  0.0 38.6 jit_solution(3888142382974470325)
XLA Ops:
  0.6 36.4 %shard_map.113.pair = f32[2,2,64,64]{3,2,1,0:T(8,128)} custom-call(f32[2,2,64,128]{3,2,1,0:T(8,128)} %fwd_prev_hbm.1, f32[2,2,64,128]{3,2,1,0:T(8,128)} %fwd_now_hbm.1, f32[2,2,64,128]{3,2,1,0:T(8,128)} %adj_late_hbm.1, f32[2,2,64,128]{3,2,1,0:T(8,128)} %adj_last_hbm.1, f32[2,64,64]{2,1,0:T(8,128)} %velocity_hbm.1, f32[1,2,64,128]{3,2,1,0:T(8,128)} %bitcast.1, ...), custom_call_target="tpu_custom_call" | custom-call | tf_op jit(solution)/shard_map/pallas_call | solution.py:491
  37.0 1.6 %shard_map.114 = (f32[2,64,64]{2,1,0:T(8,128)}, f32[2,64,64]{2,1,0:T(8,128)}) custom-call(f32[2,2,64,64]{3,2,1,0:T(8,128)} %shard_map.113.pair), custom_call_target="tpu_custom_call" | custom-call | tf_op jit(solution)/shard_map/pallas_call | solution.py:524
